TPU v7x, 32 devices: a whole 2x2x4 slice. The times are simulated.
32 devices in a mesh: seg: 2 (over x), genome: 16 (over z, y, core).
Axes of the slice: x: 2, y: 2, z: 4, core: 2. Of those that a mesh axis runs over, the one named last changes fastest.
Arguments:
- z_typed: float32 [256, 16384], P(None, ('seg', 'genome')), parts along dimension 1, may hold values from -8 to 8
- diag_inverse: float32 [32, 512, 512], P(('seg', 'genome')), parts along dimension 0
- coupling: float32 [32, 512, 256], P(('seg', 'genome')), parts along dimension 0
- impute_coef: bfloat16 [16384, 1024], P(('seg', 'genome')), parts along dimension 0, may hold values from -0.25 to 0.25
- anchor: int32 [16384], P(('seg', 'genome')), parts along dimension 0, may hold values from 0 to 8191, as said below
Outputs:
- imputed: float32 [256, 16384], P(None, ('seg', 'genome')), parts along dimension 1
There are 2 independent parts, one for each index of `seg`. A program takes and returns all parts, laid end to end along the dimension named above; each array names one. Nothing has to cross between parts.
Inputs may be any that keep to these rules, and one draw needn't show every extreme that they name: The anchor of the untyped variant t lies in typed block t // 512, i.e. in columns (t // 512) * 512 to (t // 512 + 1) * 512 - 1.
All inputs are finite; a program needn't handle non-finite values.
Results may differ from a plain program's by a relative error of at most 0.002.
The roundings to bfloat16 on the way count: a program that leaves them out, or rounds other values in their place, can miss the bound.
Values may be sent and summed in bfloat16 or wider, within the bound.
No kernel may reach another device: no remote copies, remote signals or barrier semaphores. Data moves between devices by JAX's collectives and lax.ppermute only.
A program may use at most 192 MiB of HBM per device.

v0:
```python
import functools

import jax
import jax.numpy as jnp
from jax import lax
from jax.experimental import pallas as pl
from jax.experimental.pallas import tpu as pltpu
from jax.sharding import PartitionSpec as P

AXIS = "genome"
SEGMENTS = "seg"
GROUP = 4
f32 = jnp.float32
bf16 = jnp.bfloat16
i16 = jnp.int16
SCALES = 16
LANES = 128
LIMIT = 32767.0


def parts(x):
    high = x.astype(bf16)
    return high, (x - high.astype(f32)).astype(bf16)


def dot(a, b, ca=1, cb=0):
    ah, al = parts(a)
    bh, bl = parts(b)
    return lax.dot_general(
        jnp.concatenate([al, ah, ah], axis=ca),
        jnp.concatenate([bh, bl, bh], axis=cb),
        (((ca,), (cb,)), ((), ())),
        preferred_element_type=f32,
    )


def code(x):
    top = jnp.maximum(jnp.max(jnp.abs(x), axis=0, keepdims=True), 1e-32)
    power = jnp.ceil(jnp.log2(top) * 4.0)
    root = jnp.exp2(power * -0.125)
    steps = jnp.floor(x * root * (root * LIMIT) + 0.5)
    steps = jnp.clip(steps, -LIMIT, LIMIT)
    tiles = x.shape[1] // LANES
    powers = jnp.broadcast_to(power, (SCALES // tiles, x.shape[1]))
    pieces = [v[:, i * LANES : (i + 1) * LANES] for v in (steps, powers) for i in range(tiles)]
    return jnp.concatenate(pieces, axis=0).astype(jnp.int32).astype(i16)


def decode(coded, tiles=2):
    rows = (coded.shape[0] - SCALES) // tiles
    values = coded[...].astype(jnp.int32).astype(f32)
    columns = []
    for i in range(tiles):
        at = tiles * rows + i * (SCALES // tiles)
        root = jnp.exp2(values[at : at + 1] * 0.125)
        columns.append(values[i * rows : (i + 1) * rows] * (root / LIMIT) * root)
    return jnp.concatenate(columns, axis=1)


def coded_rows(rows, columns):
    return rows * (columns // LANES) + SCALES


def where_am_i():
    place = lax.axis_index(AXIS)
    return place % 2 == 0, (place // 2) % 2 == 0, place // GROUP


def ready(b):
    bh, bl = parts(b)
    return jnp.concatenate([bh, bl, bh], axis=0)


def dot_ready(a, b):
    ah, al = parts(a)
    return jnp.dot(jnp.concatenate([al, ah, ah], axis=1), b[...], preferred_element_type=f32)


def low_traits():
    place = lax.axis_index(AXIS)
    return (place + place // 2 + place // GROUP) % 2 == 0


def ordered(first, own, other):
    return jnp.where(first, own, other), jnp.where(first, other, own)


def call(kernel, outs, *args, after=(), hbm=False, last=False, scratch=()):
    n_in, n_after = len(args), len(after)

    def body(*refs):
        kernel(*refs[:n_in], *refs[n_in + n_after :])

    single = not isinstance(outs, list)
    shapes = [outs] if single else outs
    vmem = pl.BlockSpec(memory_space=pltpu.VMEM)
    anywhere = pl.BlockSpec(memory_space=pl.ANY)
    if hbm:
        args = [pltpu.with_memory_space_constraint(a, pltpu.HBM) for a in args]
    got = pl.pallas_call(
        body,
        out_shape=[jax.ShapeDtypeStruct(s, t) if last else pltpu.VMEM(s, t) for s, t in shapes],
        in_specs=[anywhere if hbm else vmem] * n_in + [anywhere] * n_after,
        out_specs=[vmem] * len(shapes),
        scratch_shapes=scratch,
        compiler_params=pltpu.CompilerParams(vmem_limit_bytes=8 * 2**20),
        name=kernel.__name__ if hasattr(kernel, "__name__") else kernel.func.__name__,
    )(*args, *after)
    return got[0] if single else got


def tail_part(z_in, d_in, c_in, x1, s_own, z, d, c, sems):
    typed, half = c.shape
    rows = z.shape[0] // 2
    head = typed - half
    step = typed // 2
    copies = []
    for i in range(2):
        here = pl.ds(i * step, step)
        tail = (pl.ds(head, half), here)
        copies.append(pltpu.make_async_copy(d_in.at[tail], d.at[tail], sems.at[3 * i]))
        copies.append(pltpu.make_async_copy(c_in.at[here], c.at[here], sems.at[3 * i + 1]))
        copies.append(pltpu.make_async_copy(z_in.at[:, here], z.at[:, here], sems.at[3 * i + 2]))
    rest = pl.ds(0, head)
    copies.append(pltpu.make_async_copy(d_in.at[rest], d.at[rest], sems.at[6]))
    for copy in copies:
        copy.start()
    m = s = 0.0
    for i in range(2):
        here = pl.ds(i * step, step)
        for copy in copies[3 * i : 3 * i + 3]:
            copy.wait()
        tail = d[head:, here]
        m = m - dot(tail, c[here])
        s = s + dot(z[:, here], tail, 1, 1)
    x1[:half] = m
    keep, send = ordered(low_traits(), s[:rows], s[rows:])
    x1[half:] = send
    s_own[...] = keep
    copies[6].wait()


def head_part(z, d, c, x1, s_own, x3, g_own, solved, p):
    half = c.shape[1]
    rows = z.shape[0] // 2
    head = d.shape[0] - half
    first, _, _ = where_am_i()
    p[:head] = dot(d[:head], c[...])
    p[head:] = -x1[:half]
    solved[:, :head] = dot(z[...], d[:head], 1, 1)
    low, high = ordered(low_traits(), s_own[...], x1[half:])
    solved[:rows, head:] = low
    solved[rows:, head:] = high
    g = dot(solved[...], p[...])
    keep, send = ordered(low_traits(), g[:rows], g[rows:])
    x3[:half] = dot(p[...], p[...], 0, 0)
    x3[half:] = send
    g_own[...] = keep


def pair_forward(x1, got1, s_own, x2, n_own, sp_own):
    half = x1.shape[1]
    first, first_pair, _ = where_am_i()
    m0, m1 = ordered(first, x1[:half], got1[:half])
    s0, s1 = ordered(first, s_own[...], got1[half:])
    n = dot(m1, m0)
    n_own[...] = n
    split = coded_rows(half // 2, half)
    x2[:split] = code(jnp.where(first, n[: half // 2], n[half // 2 :]))
    s = dot(s0, m1, 1, 1) + s1
    rows = s.shape[0] // 2
    keep, send = ordered(first_pair, s[:rows], s[rows:])
    x2[split:] = code(send)
    sp_own[...] = keep


def pair_backward(x1, got1, s_own, x3, got3, g_own, x4, gg_own, gp_own):
    half = x1.shape[1]
    first, first_pair, _ = where_am_i()
    m0, _ = ordered(first, x1[:half], got1[:half])
    s0, _ = ordered(first, s_own[...], got1[half:])
    gg0, gg1 = ordered(first, x3[:half], got3[:half])
    g0, g1 = ordered(first, g_own[...], got3[half:])
    both = dot(jnp.concatenate([gg1, g1 - dot(s0, gg1)], axis=0), m0)
    gg = dot(m0, both[:half], 0, 0) + gg0
    gg_own[...] = gg
    split = coded_rows(half // 2, half)
    x4[:split] = code(jnp.where(first, gg[: half // 2], gg[half // 2 :]))
    g = both[half:] + g0
    rows = g.shape[0] // 2
    keep, send = ordered(first_pair, g[:rows], g[rows:])
    x4[split:] = code(send)
    gp_own[...] = keep


def pair_matrices(own, got, got_core):
    first, first_pair, _ = where_am_i()
    other = jnp.concatenate(ordered(first, got_core, got), axis=0)
    return ordered(first_pair, own[...], other)


def pair_vectors(own, got):
    _, first_pair, _ = where_am_i()
    return ordered(first_pair, own[...], got)


def relay(got, out):
    out[...] = got[: out.shape[0]]


def relay_halves(got, low, high):
    rows = low.shape[0] - SCALES
    low[:rows] = got[:rows]
    high[:rows] = got[rows : 2 * rows]
    low[rows:] = got[2 * rows : 2 * rows + SCALES]
    high[rows:] = got[2 * rows : 2 * rows + SCALES]


def group_forward(n_own, got2, got2_core, sp_own, out):
    _, _, group = where_am_i()
    out[...] = jnp.zeros_like(out)

    @pl.when(group == 0)
    def _():
        split = coded_rows(n_own.shape[1] // 2, n_own.shape[1])
        _, n1 = pair_matrices(n_own, decode(got2[:split]), decode(got2_core))
        s0, s1 = pair_vectors(sp_own, decode(got2[split:]))
        out[...] = code(dot(s0, n1, 1, 1) + s1)


def group_map(n_own, got2, got2_core, sp_own, s_group, up, down, n_first, n_second):
    split = coded_rows(n_own.shape[1] // 2, n_own.shape[1])
    n0, n1 = pair_matrices(n_own, decode(got2[:split]), decode(got2_core))
    s0, s1 = pair_vectors(sp_own, decode(got2[split:]))
    s_group[...] = dot(s0, n1, 1, 1) + s1
    n_first[...] = n0
    n_second[...] = n1
    n_group = dot(n1, n0)
    up[...] = ready(n_group.T)
    down[...] = ready(n_group)


def block_map(n_second, x1, got1, d, k):
    half = x1.shape[1]
    first, first_pair, _ = where_am_i()
    rows = lax.broadcasted_iota(jnp.int32, (half, half), 0)
    columns = lax.broadcasted_iota(jnp.int32, (half, half), 1)
    unit = (rows == columns).astype(f32)
    _, m1 = ordered(first, x1[:half], got1[:half])
    above = jnp.where(first_pair, n_second[...], unit)
    above = jnp.where(first, dot(above, m1), above)
    k[...] = dot(above, d[d.shape[0] - half :])


def group_backward(
    n_first, got2, sp_own, gg_own, got4, got4_low, got4_high, gp_own,
    gg_group, g_group, gg_second, g_second,
):
    half = n_first.shape[1]
    split = coded_rows(half // 2, half)
    n0 = n_first[...]
    s0, _ = pair_vectors(sp_own, decode(got2[split:]))
    rows = got4_low.shape[0] - SCALES
    got4_core = jnp.concatenate([got4_low[:rows], got4_high[...]], axis=0)
    gg0, gg1 = pair_matrices(gg_own, decode(got4[:split]), decode(got4_core))
    g0, g1 = pair_vectors(gp_own, decode(got4[split:]))
    gg_second[...] = gg1
    g_second[...] = g1
    both = dot(jnp.concatenate([gg1, g1 - dot(s0, gg1)], axis=0), n0)
    gg_group[...] = dot(n0, both[:half], 0, 0) + gg0
    g_group[...] = both[half:] + g0


def forward_hop(step, got, t_in, up, s_group, t_out, out):
    _, _, group = where_am_i()
    t = jnp.where(group == step + 1, decode(got), t_in[...])
    t_out[...] = t
    out[...] = code(dot_ready(t, up) + s_group[...])


def turn(step, got, t_in, gg_group, g_group, t_out, out):
    _, _, group = where_am_i()
    t = jnp.where(group == step + 1, decode(got), t_in[...])
    t_out[...] = t
    out[...] = jnp.zeros_like(out)

    @pl.when(group == step + 1)
    def _():
        out[...] = code(g_group[...] - dot(t, gg_group[...]))


def backward_hop(step, got, u_in, down, local, u_out, out):
    _, _, group = where_am_i()
    u = jnp.where(group == step, decode(got), u_in[...])
    u_out[...] = u
    out[...] = code(dot_ready(u, down) + local[...])


def arrive(step, got, u_in, out):
    _, _, group = where_am_i()
    out[...] = code(jnp.where(group == step, decode(got), u_in[...]))


def spread_forward(
    t_in, n_first, got2, sp_own, gg_second, g_second, gg_group, g_group, x5, x5_rest, kept, rest_own, local
):
    half = n_first.shape[1]
    _, first_pair, _ = where_am_i()
    s0, _ = pair_vectors(sp_own, decode(got2[coded_rows(half // 2, half) :]))
    t_mid = dot(t_in[...], n_first[...], 1, 1) + s0
    rest = g_second[...] - dot(t_mid, gg_second[...])
    keep, send = ordered(first_pair, t_in[...], t_mid)
    x5[...] = code(send)
    x5_rest[...] = code(rest)
    kept[...] = keep
    rest_own[...] = rest
    local[...] = g_group[...] - dot(t_in[...], gg_group[...])


def pair_states(kept, rest_own, got5, got5_rest, x1, got1, s_own, x3, got3, g_own, x6, own):
    half = x1.shape[1]
    rows = s_own.shape[0]
    first, first_pair, _ = where_am_i()
    t = jnp.concatenate(ordered(first_pair, kept[...], decode(got5)), axis=0)
    rest = jnp.concatenate(ordered(first_pair, rest_own[...], decode(got5_rest)), axis=0)
    m0, m1 = ordered(first, x1[:half], got1[:half])
    s0, _ = ordered(first, s_own[...], got1[half:])
    _, gg1 = ordered(first, x3[:half], got3[:half])
    _, g1 = ordered(first, g_own[...], got3[half:])
    t_mid = dot(t, m0, 1, 1) + s0
    fixed = jnp.where(first_pair, rest, 0.0)
    fixed_mid = dot(fixed, m1) + g1 - dot(t_mid, gg1)
    split = coded_rows(rows, half)
    keep, send = ordered(first, t, t_mid)
    x6[:split] = code(send)
    own[:rows] = keep
    keep, send = ordered(first, fixed_mid, fixed)
    x6[split:] = code(send)
    own[rows:] = keep


def block_parts(solved, p, d, start, maps):
    half = p.shape[1]
    start[...] = dot(solved[...], d[...])
    maps[:half] = dot(p[...], d[...], 0, 0)
    maps[half:] = d[d.shape[0] - half :]


def block_fixed(own, got6, start, maps, fixed_weights):
    rows = own.shape[0] // 2
    split = coded_rows(rows, own.shape[1])
    low = low_traits()
    t = jnp.concatenate(ordered(low, own[:rows], decode(got6[:split])), axis=0)
    above = jnp.concatenate(ordered(low, own[rows:], decode(got6[split:])), axis=0)
    fixed_weights[...] = start[...] - dot(jnp.concatenate([t, above], axis=1), maps[...])


def block_weights(mine, got_u, theirs, their_got, fixed_weights, k, xa, xb):
    half = k.shape[0]
    first, first_pair, _ = where_am_i()
    near = jnp.concatenate(ordered(first_pair, decode(mine), decode(got_u)), axis=0)
    far = jnp.concatenate(ordered(first_pair, decode(theirs), decode(their_got)), axis=0)
    u = jnp.concatenate(ordered(low_traits(), near, far), axis=0)
    weights = (fixed_weights[...] - dot(u, k[...])).astype(bf16)
    a, b = ordered(first, weights[:, :half], weights[:, half:])
    xa[...] = a
    xb[...] = b


def contract(values, coefs):
    return lax.dot_general(values, coefs, (((1,), (1,)), ((), ())), preferred_element_type=f32)


def mask_coefs(coefs_in, anchor_in, masked, coefs, anchor, sems):
    untyped, span = coefs.shape
    half = span // 4
    typed = span - 2 * half
    tile = 128
    place = lax.axis_index(AXIS)
    total = lax.axis_size(AXIS) * typed
    copies = [pltpu.make_async_copy(anchor_in, anchor, sems.at[0])]
    for i in range(untyped // tile):
        rows = pl.ds(i * tile, tile)
        copies.append(pltpu.make_async_copy(coefs_in.at[rows], coefs.at[rows], sems.at[i + 1]))
    for copy in copies:
        copy.start()
    copies[0].wait()
    first_column = place * typed - half
    for i in range(untyped // tile):
        rows = pl.ds(i * tile, tile)
        nearest = jnp.broadcast_to(anchor[:, i * tile : (i + 1) * tile], (tile, tile)).T
        copies[i + 1].wait()
        for j in range(span // tile):
            lanes = pl.ds(j * tile, tile)
            columns = first_column + j * tile + lax.broadcasted_iota(jnp.int32, (tile, tile), 1)
            within = (jnp.abs(columns - nearest) <= half) & (columns >= 0) & (columns < total)
            masked[rows, lanes] = jnp.where(within, coefs[rows, lanes].astype(f32), 0.0).astype(bf16)


def impute_own(xa, xb, masked, out):
    first, _, _ = where_am_i()
    half = xa.shape[1]
    span = masked.shape[1]
    weights = jnp.concatenate(ordered(first, xa[...], xb[...]), axis=1)
    out[...] = contract(weights, masked[:, half : span - half])


def impute_edges(acc, got_a, got_b, masked, out):
    first, _, _ = where_am_i()
    half = got_a.shape[1]
    span = masked.shape[1]
    left, right = ordered(first, got_a[...], got_b[...])
    out[...] = acc[...] + contract(left, masked[:, :half]) + contract(right, masked[:, span - half :])


def swap(block, distance):
    n = lax.axis_size(AXIS)
    return lax.ppermute(block, AXIS, [(i, i ^ distance) for i in range(n)])


def hop(block, step):
    pairs = []
    for i in range(lax.axis_size(AXIS)):
        g = i // GROUP
        to = i + GROUP if g == step else i - GROUP if g == step + 1 else i
        pairs.append((i, to ^ 1))
    return lax.ppermute(block, AXIS, pairs)


def swap_chips(block):
    n, segments = lax.axis_size(AXIS), lax.axis_size(SEGMENTS)
    pairs = []
    for seg in range(segments):
        for i in range(n):
            to, to_seg = i + 1 if i % 2 else i - 1, seg
            if not 0 <= to < n:
                to, to_seg = (i, seg ^ 1) if segments % 2 == 0 else (to % n, seg)
            pairs.append((seg * n + i, to_seg * n + to))
    return lax.ppermute(block, (SEGMENTS, AXIS), pairs)


def per_device(z, diag_inverse, coupling, impute_coef, anchor):
    d = diag_inverse[0]
    c = coupling[0]
    typed = d.shape[0]
    half = c.shape[1]
    traits = z.shape[0]
    untyped, span = impute_coef.shape
    assert span == typed + 2 * half and typed == 2 * half
    assert lax.axis_size(AXIS) >= 3 * GROUP
    groups = lax.axis_size(AXIS) // GROUP
    two, four = traits // 2, traits // 4
    square = (half, half)
    sq, h2, h4 = (square, f32), ((two, half), f32), ((four, half), f32)
    x1_shape, x6_shape = ((half + two, half), f32), ((2 * two, half), f32)
    x6_coded = ((2 * coded_rows(two, half), LANES), i16)
    coded = ((coded_rows(four, half), LANES), i16)
    coded_half = ((coded_rows(half // 2, half), LANES), i16)
    mixed = ((coded_rows(half // 2, half) + coded_rows(four, half), LANES), i16)

    solved_shape, p_shape = ((traits, typed), f32), ((typed, half), f32)
    x1, s_own, z, d, c = call(
        tail_part, [x1_shape, h2, solved_shape, ((typed, typed), f32), p_shape], z, d, c,
        hbm=True, scratch=[pltpu.SemaphoreType.DMA((7,))],
    )
    got1 = swap(x1, 1)
    x3, g_own, solved, p = call(
        head_part, [x1_shape, h2, solved_shape, p_shape], z, d, c, x1, s_own
    )
    x2, n_own, sp_own = call(pair_forward, [mixed, sq, h4], x1, got1, s_own, after=(p,))
    got2 = swap(x2, 3)
    got3 = swap(x3, 1)
    masked = call(
        mask_coefs, ((untyped, span), bf16), impute_coef, anchor[None, :], after=(x2,), hbm=True,
        scratch=[
            pltpu.VMEM((untyped, span), bf16),
            pltpu.VMEM((1, untyped), jnp.int32),
            pltpu.SemaphoreType.DMA((untyped // 128 + 1,)),
        ],
    )
    x4, gg_own, gp_own = call(
        pair_backward, [mixed, sq, h4], x1, got1, s_own, x3, got3, g_own, after=(x2,)
    )
    got2_core = swap(call(relay, coded_half, got2, after=(x4, masked)), 1)
    out = call(group_forward, coded, n_own, got2, got2_core, sp_own)
    parts3 = ((3 * half, half), bf16)
    s_group, up, down, n_first, n_second = call(
        group_map, [h4, parts3, parts3, sq, sq], n_own, got2, got2_core, sp_own, after=(out,)
    )
    k = call(block_map, ((half, typed), f32), n_second, x1, got1, d)
    t_in = jnp.zeros((four, half), f32)
    got4 = swap(x4, 3)
    for step in range(groups - 2):
        got = hop(out, step)
        t_in, out = call(
            functools.partial(forward_hop, step), [h4, coded], got, t_in, up, s_group,
            after=(k,) if step == 0 else (),
        )
        if step == 0:
            pieces = [((half // 2 + SCALES, LANES), i16)] * 2
            low, high = call(relay_halves, pieces, got4, after=(out,))
            got4_low, got4_high = swap(low, 1), swap(high, 1)
    gg_group, g_group, gg_second, g_second = call(
        group_backward, [sq, h4, sq, h4],
        n_first, got2, sp_own, gg_own, got4, got4_low, got4_high, gp_own, after=(out,),
    )
    last = groups - 2
    got = hop(out, last)
    t_in, out = call(
        functools.partial(turn, last), [h4, coded], got, t_in, gg_group, g_group
    )

    u_in = jnp.zeros((four, half), f32)
    for step in reversed(range(groups - 1)):
        got = hop(out, step)
        if step == last:
            x5, x5_rest, kept, rest_own, local = call(
                spread_forward, [coded, coded, h4, h4, h4],
                t_in, n_first, got2, sp_own, gg_second, g_second, gg_group, g_group, after=(out,),
            )
            got5, got5_rest = swap(x5, 3), swap(x5_rest, 3)
        if step:
            u_in, out = call(
                functools.partial(backward_hop, step), [h4, coded], got, u_in, down, local
            )
        else:
            start, maps = call(
                block_parts, [solved_shape, ((2 * half, typed), f32)], solved, p, d, after=(out,)
            )
            out = call(functools.partial(arrive, step), coded, got, u_in, after=(maps,))
    x6, own = call(
        pair_states, [x6_coded, x6_shape], kept, rest_own, got5, got5_rest, x1, got1, s_own, x3, got3, g_own
    )
    got6 = swap(x6, 1)
    fixed = call(block_fixed, solved_shape, own, got6, start, maps)
    theirs = swap(out, 1)
    got_u = swap(out, 3)
    their_got = swap(got_u, 1)
    edge = (square, bf16)
    xa, xb = call(block_weights, [edge, edge], out, got_u, theirs, their_got, fixed, k)
    got_a = swap_chips(xa)
    got_b = swap(xb, 1)
    acc = call(impute_own, ((traits, untyped), f32), xa, xb, masked)
    return call(
        impute_edges, ((traits, untyped), f32), acc, got_a, got_b, masked, last=True
    )


def solution(mesh):
    in_specs = (
        P(None, (SEGMENTS, AXIS)),
        P((SEGMENTS, AXIS), None, None),
        P((SEGMENTS, AXIS), None, None),
        P((SEGMENTS, AXIS), None),
        P((SEGMENTS, AXIS)),
    )
    return jax.shard_map(
        per_device, mesh=mesh, in_specs=in_specs, out_specs=P(None, (SEGMENTS, AXIS)), check_vma=False
    )
```

profile of v0, /device:TPU:1, one launch (start us, length us, event | category | flops | bytes accessed | tf_op | source)
XLA Modules:
  0.0 43.3 jit_solution(9037321431128675119)
XLA Ops:
  0.0 2.1 %tail_part.1 = (f32[384,256]{1,0:T(8,128)S(1)}, f32[128,256]{1,0:T(8,128)S(1)}, f32[256,512]{1,0:T(8,128)S(1)}, f32[512,512]{1,0:T(8,128)S(1)}, f32[512,256]{1,0:T(8,128)S(1)}) custom-call(f32[256,512]{1,0:T(8,128)} %refs_0_.2, f32[512,512]{1,0:T(8,128)} %bitcast.3, f32[512,256]{1,0:T(8,128)} %bitcast.4), custom_call_target="tpu_custom_call" | custom-call | tf_op jit(solution)/shard_map/tail_part/pallas_call | solution.py:100
  2.2 1.2 %head_part.1 = (f32[384,256]{1,0:T(8,128)S(1)}, f32[128,256]{1,0:T(8,128)S(1)}, f32[256,512]{1,0:T(8,128)S(1)}, f32[512,256]{1,0:T(8,128)S(1)}) custom-call(f32[256,512]{1,0:T(8,128)S(1)} %get-tuple-element.54.refs_0_, f32[512,512]{1,0:T(8,128)S(1)} %get-tuple-element.55.refs_1_.refs_3_.refs_2_, f32[512,256]{1,0:T(8,128)S(1)} %get-tuple-element.56.refs_2_, ...), custom_call_target="tpu_custom_call" | custom-call | tf_op jit(solution)/shard_map/head_part/pallas_call | solution.py:100
  3.4 0.5 %collective-permute-start.2 = (f32[384,256]{1,0:T(8,128)S(1)}, f32[384,256]{1,0:T(8,128)S(1)}, u32[]{:S(2)}, u32[]{:S(2)}) collective-permute-start(f32[384,256]{1,0:T(8,128)S(1)} %get-tuple-element.60.refs_3_.refs_7_), channel_id=1, source_target_pairs={{0,1},{1,0},{2,3},{3,2},{4,5},{5,4},{6,7},{7,6},{8,9},{9,8},{10,11... | collective-permute-start | bytes 1179656 | tf_op jit(solution)/shard_map/ppermute | solution.py:418
  3.9 0.5 %pair_forward.1 = (s16[416,128]{1,0:T(8,128)(2,1)S(1)}, f32[256,256]{1,0:T(8,128)S(1)}, f32[64,256]{1,0:T(8,128)S(1)}) custom-call(f32[384,256]{1,0:T(8,128)S(1)} %get-tuple-element.52.refs_3_.refs_0_.refs_1_.refs_4_, f32[384,256]{1,0:T(8,128)S(1)} %collective-permute-done.refs_1_.refs_2_.refs_5_, f32[128,256]{1,0:T(8,128)S(1)} %get-tuple-element.53.refs_4_.refs_2_.refs_6_, ...), custom_call_target="tpu_custom_call" | custom-call | tf_op jit(solution)/shard_map/pair_forward/pallas_call | solution.py:100
  4.4 2.7 %collective-permute-start.1 = (s16[416,128]{1,0:T(8,128)(2,1)S(1)}, s16[416,128]{1,0:T(8,128)(2,1)S(1)}, u32[]{:S(2)}, u32[]{:S(2)}) collective-permute-start(s16[416,128]{1,0:T(8,128)(2,1)S(1)} %get-tuple-element.59.refs_6_.refs_2_), channel_id=1, source_target_pairs={{0,3},{1,2},{2,1},{3,0},{4,7},{5,6},{6,5},{7,4},{8,11},{9,10},{10,... | collective-permute-start | bytes 319496 | tf_op jit(solution)/shard_map/ppermute | solution.py:418
  7.1 1.7 %mask_coefs.1.refs_2_.refs_3_ = bf16[512,1024]{1,0:T(8,128)(2,1)S(1)} custom-call(bf16[512,1024]{1,0:T(8,128)(2,1)} %refs_0_.3, s32[1,512]{1,0:T(1,128)} %bitcast.5, s16[416,128]{1,0:T(8,128)(2,1)S(1)} %get-tuple-element.59.refs_6_.refs_2_), custom_call_target="tpu_custom_call" | custom-call | tf_op jit(solution)/shard_map/mask_coefs/pallas_call | solution.py:100
  8.8 1.0 %pair_backward.1 = (s16[416,128]{1,0:T(8,128)(2,1)S(1)}, f32[256,256]{1,0:T(8,128)S(1)}, f32[64,256]{1,0:T(8,128)S(1)}) custom-call(f32[384,256]{1,0:T(8,128)S(1)} %get-tuple-element.52.refs_3_.refs_0_.refs_1_.refs_4_, f32[384,256]{1,0:T(8,128)S(1)} %collective-permute-done.refs_1_.refs_2_.refs_5_, f32[128,256]{1,0:T(8,128)S(1)} %get-tuple-element.53.refs_4_.refs_2_.refs_6_, ...), custom_call_target="tpu_custom_call" | custom-call | tf_op jit(solution)/shard_map/pair_backward/pallas_call | solution.py:100
  9.8 0.2 collective-permute-done.1.refs_0_.refs_1_.refs_2_
  10.0 0.3 collective-permute-start.3
  10.3 2.0 %collective-permute-start.7 = (s16[416,128]{1,0:T(8,128)(2,1)S(1)}, s16[416,128]{1,0:T(8,128)(2,1)S(1)}, u32[]{:S(2)}, u32[]{:S(2)}) collective-permute-start(s16[416,128]{1,0:T(8,128)(2,1)S(1)} %get-tuple-element.62.refs_1_), channel_id=1, source_target_pairs={{0,3},{1,2},{2,1},{3,0},{4,7},{5,6},{6,5},{7,4},{8,11},{9,10},{10,... | collective-permute-start | bytes 319496 | tf_op jit(solution)/shard_map/ppermute | solution.py:418
  12.3 0.4 group_forward.1.refs_4_
  12.7 1.3 %collective-permute-start.4 = (s16[144,128]{1,0:T(8,128)(2,1)S(1)}, s16[144,128]{1,0:T(8,128)(2,1)S(1)}, u32[]{:S(2)}, u32[]{:S(2)}) collective-permute-start(s16[144,128]{1,0:T(8,128)(2,1)S(1)} %group_forward.1.refs_4_), channel_id=1, source_target_pairs={{0,5},{1,4},{2,7},{3,6},{4,1},{5,0},{6,3},{7,2},{8,9},{9,8},{10,11... | collective-permute-start | bytes 110600 | tf_op jit(solution)/shard_map/ppermute | solution.py:427
  13.9 0.5 %group_map.1 = (f32[64,256]{1,0:T(8,128)S(1)}, bf16[768,256]{1,0:T(8,128)(2,1)S(1)}, bf16[768,256]{1,0:T(8,128)(2,1)S(1)}, f32[256,256]{1,0:T(8,128)S(1)}, f32[256,256]{1,0:T(8,128)S(1)}) custom-call(f32[256,256]{1,0:T(8,128)S(1)} %get-tuple-element.58.refs_0_, s16[416,128]{1,0:T(8,128)(2,1)S(1)} %collective-permute-done.1.refs_0_.refs_1_.refs_2_, ...), custom_call_target="tpu_custom_call" | custom-call | tf_op jit(solution)/shard_map/group_map/pallas_call | solution.py:100
  14.4 0.6 %block_map.1.refs_4_.refs_5_ = f32[256,512]{1,0:T(8,128)S(1)} custom-call(f32[256,256]{1,0:T(8,128)S(1)} %get-tuple-element.66.refs_0_, f32[384,256]{1,0:T(8,128)S(1)} %get-tuple-element.52.refs_3_.refs_0_.refs_1_.refs_4_, f32[384,256]{1,0:T(8,128)S(1)} %collective-permute-done.refs_1_.refs_2_.refs_5_, f32[512,512]{1,0:T(8,128)S(1)} %get-tuple-element.55.refs_1_.refs_3_.refs_2_), custom_call_target="tpu_custom_call" | custom-call | tf_op jit(solution)/shard_map/block_map/pallas_call | solution.py:100
  15.0 1.2 %collective-permute-done.4.refs_0_ = s16[144,128]{1,0:T(8,128)(2,1)S(1)} collective-permute-done((s16[144,128]{1,0:T(8,128)(2,1)S(1)}, s16[144,128]{1,0:T(8,128)(2,1)S(1)}, u32[]{:S(2)}, u32[]{:S(2)}) %collective-permute-start.4) | collective-permute-done | bytes 36896 | tf_op jit(solution)/shard_map/ppermute | solution.py:427
  16.2 0.2 forward_hop.2
  16.4 0.4 collective-permute-start.5
  16.9 0.2 collective-permute-start.8
  17.1 0.4 collective-permute-start.9
  17.4 0.3 collective-permute-done.5.refs_0_
  17.7 0.2 forward_hop.3
  18.0 0.4 collective-permute-start.6
  18.4 0.9 %group_backward.1 = (f32[256,256]{1,0:T(8,128)S(1)}, f32[64,256]{1,0:T(8,128)S(1)}, f32[256,256]{1,0:T(8,128)S(1)}, f32[64,256]{1,0:T(8,128)S(1)}) custom-call(f32[256,256]{1,0:T(8,128)S(1)} %get-tuple-element.71.refs_0_.refs_1_, s16[416,128]{1,0:T(8,128)(2,1)S(1)} %collective-permute-done.1.refs_0_.refs_1_.refs_2_, ...), custom_call_target="tpu_custom_call" | custom-call | tf_op jit(solution)/shard_map/group_backward/pallas_call | solution.py:100
  19.3 0.4 collective-permute-start.10
  19.7 0.6 %spread_forward.1 = (s16[144,128]{1,0:T(8,128)(2,1)S(1)}, s16[144,128]{1,0:T(8,128)(2,1)S(1)}, f32[64,256]{1,0:T(8,128)S(1)}, f32[64,256]{1,0:T(8,128)S(1)}, f32[64,256]{1,0:T(8,128)S(1)}) custom-call(f32[64,256]{1,0:T(8,128)S(1)} %get-tuple-element.80.refs_0_, f32[256,256]{1,0:T(8,128)S(1)} %get-tuple-element.71.refs_0_.refs_1_, ...), custom_call_target="tpu_custom_call" | custom-call | tf_op jit(solution)/shard_map/spread_forward/pallas_call | solution.py:100
  20.3 1.0 %collective-permute-start.16 = (s16[144,128]{1,0:T(8,128)(2,1)S(1)}, s16[144,128]{1,0:T(8,128)(2,1)S(1)}, u32[]{:S(2)}, u32[]{:S(2)}) collective-permute-start(s16[144,128]{1,0:T(8,128)(2,1)S(1)} %get-tuple-element.92), channel_id=1, source_target_pairs={{0,3},{1,2},{2,1},{3,0},{4,7},{5,6},{6,5},{7,4},{8,11},{9,10},{10,... | collective-permute-start | bytes 110600 | tf_op jit(solution)/shard_map/ppermute | solution.py:418
  21.4 0.8 %collective-permute-start.17 = (s16[144,128]{1,0:T(8,128)(2,1)S(1)}, s16[144,128]{1,0:T(8,128)(2,1)S(1)}, u32[]{:S(2)}, u32[]{:S(2)}) collective-permute-start(s16[144,128]{1,0:T(8,128)(2,1)S(1)} %get-tuple-element.93), channel_id=1, source_target_pairs={{0,3},{1,2},{2,1},{3,0},{4,7},{5,6},{6,5},{7,4},{8,11},{9,10},{10,... | collective-permute-start | bytes 110600 | tf_op jit(solution)/shard_map/ppermute | solution.py:418
  22.2 0.2 backward_hop.2
  22.4 0.3 collective-permute-start.11
  22.7 1.1 %collective-permute-done.16.refs_2_ = s16[144,128]{1,0:T(8,128)(2,1)S(1)} collective-permute-done((s16[144,128]{1,0:T(8,128)(2,1)S(1)}, s16[144,128]{1,0:T(8,128)(2,1)S(1)}, u32[]{:S(2)}, u32[]{:S(2)}) %collective-permute-start.16) | collective-permute-done | bytes 36896 | tf_op jit(solution)/shard_map/ppermute | solution.py:418
  23.8 1.0 %collective-permute-done.17.refs_3_ = s16[144,128]{1,0:T(8,128)(2,1)S(1)} collective-permute-done((s16[144,128]{1,0:T(8,128)(2,1)S(1)}, s16[144,128]{1,0:T(8,128)(2,1)S(1)}, u32[]{:S(2)}, u32[]{:S(2)}) %collective-permute-start.17) | collective-permute-done | bytes 36896 | tf_op jit(solution)/shard_map/ppermute | solution.py:418
  24.7 0.7 %pair_states.1 = (s16[544,128]{1,0:T(8,128)(2,1)S(1)}, f32[256,256]{1,0:T(8,128)S(1)}) custom-call(f32[64,256]{1,0:T(8,128)S(1)} %get-tuple-element.90.refs_0_, f32[64,256]{1,0:T(8,128)S(1)} %get-tuple-element.91.refs_1_, s16[144,128]{1,0:T(8,128)(2,1)S(1)} %collective-permute-done.16.refs_2_, s16[144,128]{1,0:T(8,128)(2,1)S(1)} %collective-permute-done.17.refs_3_, ...), custom_call_target="tpu_custom_call" | custom-call | tf_op jit(solution)/shard_map/pair_states/pallas_call | solution.py:100
  25.4 0.4 collective-permute-start.18
  25.8 0.2 backward_hop.3
  26.0 4.6 %collective-permute-start.12 = (s16[144,128]{1,0:T(8,128)(2,1)S(1)}, s16[144,128]{1,0:T(8,128)(2,1)S(1)}, u32[]{:S(2)}, u32[]{:S(2)}) collective-permute-start(s16[144,128]{1,0:T(8,128)(2,1)S(1)} %get-tuple-element.86.refs_3_), channel_id=1, source_target_pairs={{0,5},{1,4},{2,7},{3,6},{4,1},{5,0},{6,3},{7,2},{8,9},{9,8},{10,11... | collective-permute-start | bytes 110600 | tf_op jit(solution)/shard_map/ppermute | solution.py:427
  30.6 1.1 %block_parts.1 = (f32[256,512]{1,0:T(8,128)S(1)}, f32[512,512]{1,0:T(8,128)S(1)}) custom-call(f32[256,512]{1,0:T(8,128)S(1)} %get-tuple-element.88.refs_0_, f32[512,256]{1,0:T(8,128)S(1)} %get-tuple-element.57.refs_3_.refs_1_, f32[512,512]{1,0:T(8,128)S(1)} %get-tuple-element.55.refs_1_.refs_3_.refs_2_, s16[144,128]{1,0:T(8,128)(2,1)S(1)} %get-tuple-element.86.refs_3_), custom_call_target="tpu_custom_call" | custom-call | tf_op jit(solution)/shard_map/block_parts/pallas_call | solution.py:100
  31.7 0.6 %collective-permute-done.12.refs_0_ = s16[144,128]{1,0:T(8,128)(2,1)S(1)} collective-permute-done((s16[144,128]{1,0:T(8,128)(2,1)S(1)}, s16[144,128]{1,0:T(8,128)(2,1)S(1)}, u32[]{:S(2)}, u32[]{:S(2)}) %collective-permute-start.12) | collective-permute-done | bytes 36896 | tf_op jit(solution)/shard_map/ppermute | solution.py:427
  32.3 1.2 %collective-permute-start.13 = (s16[144,128]{1,0:T(8,128)(2,1)S(1)}, s16[144,128]{1,0:T(8,128)(2,1)S(1)}, u32[]{:S(2)}, u32[]{:S(2)}) collective-permute-start(s16[144,128]{1,0:T(8,128)(2,1)S(1)} %arrive.1.refs_0_), channel_id=1, source_target_pairs={{0,3},{1,2},{2,1},{3,0},{4,7},{5,6},{6,5},{7,4},{8,11},{9,10},{10,... | collective-permute-start | bytes 110600 | tf_op jit(solution)/shard_map/ppermute | solution.py:418
  33.7 2.0 %collective-permute-done.13.refs_1_ = s16[144,128]{1,0:T(8,128)(2,1)S(1)} collective-permute-done((s16[144,128]{1,0:T(8,128)(2,1)S(1)}, s16[144,128]{1,0:T(8,128)(2,1)S(1)}, u32[]{:S(2)}, u32[]{:S(2)}) %collective-permute-start.13) | collective-permute-done | bytes 36896 | tf_op jit(solution)/shard_map/ppermute | solution.py:418
  35.8 0.2 collective-permute-start.15
  35.9 0.7 %block_fixed.1.refs_4_ = f32[256,512]{1,0:T(8,128)S(1)} custom-call(f32[256,256]{1,0:T(8,128)S(1)} %get-tuple-element.94.refs_0_, s16[544,128]{1,0:T(8,128)(2,1)S(1)} %collective-permute-done.18.refs_1_, f32[256,512]{1,0:T(8,128)S(1)} %get-tuple-element.96.refs_2_, f32[512,512]{1,0:T(8,128)S(1)} %get-tuple-element.89.refs_2_.refs_3_), custom_call_target="tpu_custom_call" | custom-call | tf_op jit(solution)/shard_map/block_fixed/pallas_call | solution.py:100
  36.6 0.4 collective-permute-done.15.refs_3_
  37.0 0.4 block_weights.1
  37.4 1.3 %collective-permute-start.19 = (bf16[256,256]{1,0:T(8,128)(2,1)S(1)}, bf16[256,256]{1,0:T(8,128)(2,1)S(1)}, u32[]{:S(2)}, u32[]{:S(2)}) collective-permute-start(bf16[256,256]{1,0:T(8,128)(2,1)S(1)} %get-tuple-element.97.refs_0_), channel_id=1, source_target_pairs={{0,16},{1,2},{2,1},{3,4},{4,3},{5,6},{6,5},{7,8},{8,7},{9,10},{10,... | collective-permute-start | bytes 393224 | tf_op jit(solution)/shard_map/ppermute | solution.py:439
  38.7 0.4 collective-permute-start.20
  39.1 0.3 impute_own.1.refs_0_
  39.5 2.7 %collective-permute-done.19.refs_1_ = bf16[256,256]{1,0:T(8,128)(2,1)S(1)} collective-permute-done((bf16[256,256]{1,0:T(8,128)(2,1)S(1)}, bf16[256,256]{1,0:T(8,128)(2,1)S(1)}, u32[]{:S(2)}, u32[]{:S(2)}) %collective-permute-start.19) | collective-permute-done | bytes 131104 | tf_op jit(solution)/shard_map/ppermute | solution.py:439
  42.2 1.1 %impute_edges.1 = f32[256,512]{1,0:T(8,128)} custom-call(f32[256,512]{1,0:T(8,128)S(1)} %impute_own.1.refs_0_, bf16[256,256]{1,0:T(8,128)(2,1)S(1)} %collective-permute-done.19.refs_1_, bf16[256,256]{1,0:T(8,128)(2,1)S(1)} %collective-permute-done.20.refs_2_, bf16[512,1024]{1,0:T(8,128)(2,1)S(1)} %mask_coefs.1.refs_2_.refs_3_), custom_call_target="tpu_custom_call" | custom-call | tf_op jit(solution)/shard_map/impute_edges/pallas_call | solution.py:100
  (19 shorter events, 0.4 us)
Async XLA Ops:
  2.1 1.9 %collective-permute-start = (f32[384,256]{1,0:T(8,128)S(1)}, f32[384,256]{1,0:T(8,128)S(1)}, u32[]{:S(2)}, u32[]{:S(2)}) collective-permute-start(f32[384,256]{1,0:T(8,128)S(1)} %get-tuple-element.52.refs_3_.refs_0_.refs_1_.refs_4_), channel_id=1, source_target_pairs={{0,1},{1,0},{2,3},{3,2},{4,5},{5,4},{6,7},{7,6},{8,9},{9,8},{10,11... | collective-permute-start | bytes 1179656 | tf_op jit(solution)/shard_map/ppermute | solution.py:418
  3.4 5.4 %collective-permute-start.2 = (f32[384,256]{1,0:T(8,128)S(1)}, f32[384,256]{1,0:T(8,128)S(1)}, u32[]{:S(2)}, u32[]{:S(2)}) collective-permute-start(f32[384,256]{1,0:T(8,128)S(1)} %get-tuple-element.60.refs_3_.refs_7_), channel_id=1, source_target_pairs={{0,1},{1,0},{2,3},{3,2},{4,5},{5,4},{6,7},{7,6},{8,9},{9,8},{10,11... | collective-permute-start | bytes 1179656 | tf_op jit(solution)/shard_map/ppermute | solution.py:418
  4.4 5.6 %collective-permute-start.1 = (s16[416,128]{1,0:T(8,128)(2,1)S(1)}, s16[416,128]{1,0:T(8,128)(2,1)S(1)}, u32[]{:S(2)}, u32[]{:S(2)}) collective-permute-start(s16[416,128]{1,0:T(8,128)(2,1)S(1)} %get-tuple-element.59.refs_6_.refs_2_), channel_id=1, source_target_pairs={{0,3},{1,2},{2,1},{3,0},{4,7},{5,6},{6,5},{7,4},{8,11},{9,10},{10,... | collective-permute-start | bytes 319496 | tf_op jit(solution)/shard_map/ppermute | solution.py:418
  10.0 2.3 %collective-permute-start.3 = (s16[272,128]{1,0:T(8,128)(2,1)S(1)}, s16[272,128]{1,0:T(8,128)(2,1)S(1)}, u32[]{:S(2)}, u32[]{:S(2)}) collective-permute-start(s16[272,128]{1,0:T(8,128)(2,1)S(1)} %relay.1), channel_id=1, source_target_pairs={{0,1},{1,0},{2,3},{3,2},{4,5},{5,4},{6,7},{7,6},{8,9},{9,8},{10,11... | collective-permute-start | bytes 208904 | tf_op jit(solution)/shard_map/ppermute | solution.py:418
  10.3 6.6 %collective-permute-start.7 = (s16[416,128]{1,0:T(8,128)(2,1)S(1)}, s16[416,128]{1,0:T(8,128)(2,1)S(1)}, u32[]{:S(2)}, u32[]{:S(2)}) collective-permute-start(s16[416,128]{1,0:T(8,128)(2,1)S(1)} %get-tuple-element.62.refs_1_), channel_id=1, source_target_pairs={{0,3},{1,2},{2,1},{3,0},{4,7},{5,6},{6,5},{7,4},{8,11},{9,10},{10,... | collective-permute-start | bytes 319496 | tf_op jit(solution)/shard_map/ppermute | solution.py:418
  12.7 3.5 %collective-permute-start.4 = (s16[144,128]{1,0:T(8,128)(2,1)S(1)}, s16[144,128]{1,0:T(8,128)(2,1)S(1)}, u32[]{:S(2)}, u32[]{:S(2)}) collective-permute-start(s16[144,128]{1,0:T(8,128)(2,1)S(1)} %group_forward.1.refs_4_), channel_id=1, source_target_pairs={{0,5},{1,4},{2,7},{3,6},{4,1},{5,0},{6,3},{7,2},{8,9},{9,8},{10,11... | collective-permute-start | bytes 110600 | tf_op jit(solution)/shard_map/ppermute | solution.py:427
  16.4 1.3 %collective-permute-start.5 = (s16[144,128]{1,0:T(8,128)(2,1)S(1)}, s16[144,128]{1,0:T(8,128)(2,1)S(1)}, u32[]{:S(2)}, u32[]{:S(2)}) collective-permute-start(s16[144,128]{1,0:T(8,128)(2,1)S(1)} %get-tuple-element.67.refs_1_), channel_id=1, source_target_pairs={{0,1},{1,0},{2,3},{3,2},{4,9},{5,8},{6,11},{7,10},{8,5},{9,4},{10,... | collective-permute-start | bytes 110600 | tf_op jit(solution)/shard_map/ppermute | solution.py:427
  16.9 1.5 %collective-permute-start.8 = (s16[144,128]{1,0:T(8,128)(2,1)S(1)}, s16[144,128]{1,0:T(8,128)(2,1)S(1)}, u32[]{:S(2)}, u32[]{:S(2)}) collective-permute-start(s16[144,128]{1,0:T(8,128)(2,1)S(1)} %get-tuple-element.73), channel_id=1, source_target_pairs={{0,1},{1,0},{2,3},{3,2},{4,5},{5,4},{6,7},{7,6},{8,9},{9,8},{10,11... | collective-permute-start | bytes 110600 | tf_op jit(solution)/shard_map/ppermute | solution.py:418
  17.1 1.3 %collective-permute-start.9 = (s16[144,128]{1,0:T(8,128)(2,1)S(1)}, s16[144,128]{1,0:T(8,128)(2,1)S(1)}, u32[]{:S(2)}, u32[]{:S(2)}) collective-permute-start(s16[144,128]{1,0:T(8,128)(2,1)S(1)} %get-tuple-element.74), channel_id=1, source_target_pairs={{0,1},{1,0},{2,3},{3,2},{4,5},{5,4},{6,7},{7,6},{8,9},{9,8},{10,11... | collective-permute-start | bytes 110600 | tf_op jit(solution)/shard_map/ppermute | solution.py:418
  18.0 1.3 %collective-permute-start.6 = (s16[144,128]{1,0:T(8,128)(2,1)S(1)}, s16[144,128]{1,0:T(8,128)(2,1)S(1)}, u32[]{:S(2)}, u32[]{:S(2)}) collective-permute-start(s16[144,128]{1,0:T(8,128)(2,1)S(1)} %get-tuple-element.69.refs_8_), channel_id=1, source_target_pairs={{0,1},{1,0},{2,3},{3,2},{4,5},{5,4},{6,7},{7,6},{8,13},{9,12},{10,... | collective-permute-start | bytes 110600 | tf_op jit(solution)/shard_map/ppermute | solution.py:427
  19.3 2.8 %collective-permute-start.10 = (s16[144,128]{1,0:T(8,128)(2,1)S(1)}, s16[144,128]{1,0:T(8,128)(2,1)S(1)}, u32[]{:S(2)}, u32[]{:S(2)}) collective-permute-start(s16[144,128]{1,0:T(8,128)(2,1)S(1)} %get-tuple-element.78.refs_8_), channel_id=1, source_target_pairs={{0,1},{1,0},{2,3},{3,2},{4,5},{5,4},{6,7},{7,6},{8,13},{9,12},{10,... | collective-permute-start | bytes 110600 | tf_op jit(solution)/shard_map/ppermute | solution.py:427
  20.3 3.4 %collective-permute-start.16 = (s16[144,128]{1,0:T(8,128)(2,1)S(1)}, s16[144,128]{1,0:T(8,128)(2,1)S(1)}, u32[]{:S(2)}, u32[]{:S(2)}) collective-permute-start(s16[144,128]{1,0:T(8,128)(2,1)S(1)} %get-tuple-element.92), channel_id=1, source_target_pairs={{0,3},{1,2},{2,1},{3,0},{4,7},{5,6},{6,5},{7,4},{8,11},{9,10},{10,... | collective-permute-start | bytes 110600 | tf_op jit(solution)/shard_map/ppermute | solution.py:418
  21.4 3.4 %collective-permute-start.17 = (s16[144,128]{1,0:T(8,128)(2,1)S(1)}, s16[144,128]{1,0:T(8,128)(2,1)S(1)}, u32[]{:S(2)}, u32[]{:S(2)}) collective-permute-start(s16[144,128]{1,0:T(8,128)(2,1)S(1)} %get-tuple-element.93), channel_id=1, source_target_pairs={{0,3},{1,2},{2,1},{3,0},{4,7},{5,6},{6,5},{7,4},{8,11},{9,10},{10,... | collective-permute-start | bytes 110600 | tf_op jit(solution)/shard_map/ppermute | solution.py:418
  22.4 3.4 %collective-permute-start.11 = (s16[144,128]{1,0:T(8,128)(2,1)S(1)}, s16[144,128]{1,0:T(8,128)(2,1)S(1)}, u32[]{:S(2)}, u32[]{:S(2)}) collective-permute-start(s16[144,128]{1,0:T(8,128)(2,1)S(1)} %get-tuple-element.84), channel_id=1, source_target_pairs={{0,1},{1,0},{2,3},{3,2},{4,9},{5,8},{6,11},{7,10},{8,5},{9,4},{10,... | collective-permute-start | bytes 110600 | tf_op jit(solution)/shard_map/ppermute | solution.py:427
  25.4 10.5 %collective-permute-start.18 = (s16[544,128]{1,0:T(8,128)(2,1)S(1)}, s16[544,128]{1,0:T(8,128)(2,1)S(1)}, u32[]{:S(2)}, u32[]{:S(2)}) collective-permute-start(s16[544,128]{1,0:T(8,128)(2,1)S(1)} %get-tuple-element.95), channel_id=1, source_target_pairs={{0,1},{1,0},{2,3},{3,2},{4,5},{5,4},{6,7},{7,6},{8,9},{9,8},{10,11... | collective-permute-start | bytes 417800 | tf_op jit(solution)/shard_map/ppermute | solution.py:418
  26.0 6.2 %collective-permute-start.12 = (s16[144,128]{1,0:T(8,128)(2,1)S(1)}, s16[144,128]{1,0:T(8,128)(2,1)S(1)}, u32[]{:S(2)}, u32[]{:S(2)}) collective-permute-start(s16[144,128]{1,0:T(8,128)(2,1)S(1)} %get-tuple-element.86.refs_3_), channel_id=1, source_target_pairs={{0,5},{1,4},{2,7},{3,6},{4,1},{5,0},{6,3},{7,2},{8,9},{9,8},{10,11... | collective-permute-start | bytes 110600 | tf_op jit(solution)/shard_map/ppermute | solution.py:427
  32.3 3.4 %collective-permute-start.13 = (s16[144,128]{1,0:T(8,128)(2,1)S(1)}, s16[144,128]{1,0:T(8,128)(2,1)S(1)}, u32[]{:S(2)}, u32[]{:S(2)}) collective-permute-start(s16[144,128]{1,0:T(8,128)(2,1)S(1)} %arrive.1.refs_0_), channel_id=1, source_target_pairs={{0,3},{1,2},{2,1},{3,0},{4,7},{5,6},{6,5},{7,4},{8,11},{9,10},{10,... | collective-permute-start | bytes 110600 | tf_op jit(solution)/shard_map/ppermute | solution.py:418
  33.5 3.0 %collective-permute-start.14 = (s16[144,128]{1,0:T(8,128)(2,1)S(1)}, s16[144,128]{1,0:T(8,128)(2,1)S(1)}, u32[]{:S(2)}, u32[]{:S(2)}) collective-permute-start(s16[144,128]{1,0:T(8,128)(2,1)S(1)} %arrive.1.refs_0_), channel_id=1, source_target_pairs={{0,1},{1,0},{2,3},{3,2},{4,5},{5,4},{6,7},{7,6},{8,9},{9,8},{10,11... | collective-permute-start | bytes 110600 | tf_op jit(solution)/shard_map/ppermute | solution.py:418
  35.8 1.2 %collective-permute-start.15 = (s16[144,128]{1,0:T(8,128)(2,1)S(1)}, s16[144,128]{1,0:T(8,128)(2,1)S(1)}, u32[]{:S(2)}, u32[]{:S(2)}) collective-permute-start(s16[144,128]{1,0:T(8,128)(2,1)S(1)} %collective-permute-done.13.refs_1_), channel_id=1, source_target_pairs={{0,1},{1,0},{2,3},{3,2},{4,5},{5,4},{6,7},{7,6},{8,9},{9,8},{10,11... | collective-permute-start | bytes 110600 | tf_op jit(solution)/shard_map/ppermute | solution.py:418
  37.4 4.8 %collective-permute-start.19 = (bf16[256,256]{1,0:T(8,128)(2,1)S(1)}, bf16[256,256]{1,0:T(8,128)(2,1)S(1)}, u32[]{:S(2)}, u32[]{:S(2)}) collective-permute-start(bf16[256,256]{1,0:T(8,128)(2,1)S(1)} %get-tuple-element.97.refs_0_), channel_id=1, source_target_pairs={{0,16},{1,2},{2,1},{3,4},{4,3},{5,6},{6,5},{7,8},{8,7},{9,10},{10,... | collective-permute-start | bytes 393224 | tf_op jit(solution)/shard_map/ppermute | solution.py:439
  38.7 3.5 %collective-permute-start.20 = (bf16[256,256]{1,0:T(8,128)(2,1)S(1)}, bf16[256,256]{1,0:T(8,128)(2,1)S(1)}, u32[]{:S(2)}, u32[]{:S(2)}) collective-permute-start(bf16[256,256]{1,0:T(8,128)(2,1)S(1)} %get-tuple-element.98.refs_1_), channel_id=1, source_target_pairs={{0,1},{1,0},{2,3},{3,2},{4,5},{5,4},{6,7},{7,6},{8,9},{9,8},{10,11... | collective-permute-start | bytes 393224 | tf_op jit(solution)/shard_map/ppermute | solution.py:418
where the time goes:
time: 44 us; the launch traced here: 43.3 us
  starting transfers between devices  19 us (43%)
  Pallas kernels  14.7 us (33%)
  waiting for transfers between devices  9.38 us (21%)
    pallas_call x24, Pallas kernels, call(): pl.pallas_call(body, out_shape=[jax.ShapeDtypeStruct(s, t) if last else p...  14.7 us
    ppermute x14, starting transfers between devices, swap(): return lax.ppermute(block, AXIS, [(i, i ^ distance) for i in range(n)])  10.3 us
    ppermute x6, starting transfers between devices, hop(): return lax.ppermute(block, AXIS, pairs)  7.33 us
    ppermute x14, waiting for transfers between devices, swap(): return lax.ppermute(block, AXIS, [(i, i ^ distance) for i in range(n)])  4.67 us
    ppermute x1, waiting for transfers between devices, swap_chips(): return lax.ppermute(block, (SEGMENTS, AXIS), pairs)  2.69 us
    ppermute x6, waiting for transfers between devices, hop(): return lax.ppermute(block, AXIS, pairs)  2.02 us
    ppermute x1, starting transfers between devices, swap_chips(): return lax.ppermute(block, (SEGMENTS, AXIS), pairs)  1.3 us
  transfers between devices with their start and end apart: 21, of which 9 were waited for; matrix products, arithmetic and copies ran while one was open for 0% of the time, Pallas kernels for 26%

commit v1 on v0

--- a/solution.py
+++ b/solution.py
@@ -174,7 +174,21 @@
     sp_own[...] = keep
 
 
-def pair_backward(x1, got1, s_own, x3, got3, g_own, x4, gg_own, gp_own):
+def packed(m):
+    half, quarter = m.shape[0] // 2, m.shape[0] // 4
+    corner = m[half:, half:]
+    low = jnp.concatenate([corner[:quarter], corner[quarter:]], axis=1)
+    return jnp.concatenate([m[:half], low], axis=0)
+
+
+def unpacked(rows):
+    half = rows.shape[1] // 2
+    corner = jnp.concatenate([rows[half:, :half], rows[half:, half:]], axis=0)
+    low = jnp.concatenate([rows[:half, half:].T, corner], axis=1)
+    return jnp.concatenate([rows[:half], low], axis=0)
+
+
+def pair_backward(x1, got1, s_own, x3, got3, g_own, x4, x4_low, gg_own, gp_own):
     half = x1.shape[1]
     first, first_pair, _ = where_am_i()
     m0, _ = ordered(first, x1[:half], got1[:half])
@@ -184,12 +198,14 @@
     both = dot(jnp.concatenate([gg1, g1 - dot(s0, gg1)], axis=0), m0)
     gg = dot(m0, both[:half], 0, 0) + gg0
     gg_own[...] = gg
-    split = coded_rows(half // 2, half)
-    x4[:split] = code(jnp.where(first, gg[: half // 2], gg[half // 2 :]))
+    rows = packed(gg)
+    split = coded_rows(half // 4, half)
+    x4[...] = code(rows[: half // 2])
+    x4_low[:split] = code(rows[half // 2 :])
     g = both[half:] + g0
     rows = g.shape[0] // 2
     keep, send = ordered(first_pair, g[:rows], g[rows:])
-    x4[split:] = code(send)
+    x4_low[split:] = code(send)
     gp_own[...] = keep
 
 
@@ -206,14 +222,6 @@
 
 def relay(got, out):
     out[...] = got[: out.shape[0]]
-
-
-def relay_halves(got, low, high):
-    rows = low.shape[0] - SCALES
-    low[:rows] = got[:rows]
-    high[:rows] = got[rows : 2 * rows]
-    low[rows:] = got[2 * rows : 2 * rows + SCALES]
-    high[rows:] = got[2 * rows : 2 * rows + SCALES]
 
 
 def group_forward(n_own, got2, got2_core, sp_own, out):
@@ -253,17 +261,16 @@
 
 
 def group_backward(
-    n_first, got2, sp_own, gg_own, got4, got4_low, got4_high, gp_own,
-    gg_group, g_group, gg_second, g_second,
+    n_first, got2, sp_own, gg_own, got4, got4_low, gp_own, gg_group, g_group, gg_second, g_second
 ):
     half = n_first.shape[1]
-    split = coded_rows(half // 2, half)
+    split = coded_rows(half // 4, half)
+    _, first_pair, _ = where_am_i()
     n0 = n_first[...]
-    s0, _ = pair_vectors(sp_own, decode(got2[split:]))
-    rows = got4_low.shape[0] - SCALES
-    got4_core = jnp.concatenate([got4_low[:rows], got4_high[...]], axis=0)
-    gg0, gg1 = pair_matrices(gg_own, decode(got4[:split]), decode(got4_core))
-    g0, g1 = pair_vectors(gp_own, decode(got4[split:]))
+    s0, _ = pair_vectors(sp_own, decode(got2[coded_rows(half // 2, half) :]))
+    other = jnp.concatenate([decode(got4), decode(got4_low[:split])], axis=0)
+    gg0, gg1 = ordered(first_pair, gg_own[...], unpacked(other))
+    g0, g1 = pair_vectors(gp_own, decode(got4_low[split:]))
     gg_second[...] = gg1
     g_second[...] = g1
     both = dot(jnp.concatenate([gg1, g1 - dot(s0, gg1)], axis=0), n0)
@@ -456,6 +463,7 @@
     x6_coded = ((2 * coded_rows(two, half), LANES), i16)
     coded = ((coded_rows(four, half), LANES), i16)
     coded_half = ((coded_rows(half // 2, half), LANES), i16)
+    two_coded = ((2 * coded_rows(four, half), LANES), i16)
     mixed = ((coded_rows(half // 2, half) + coded_rows(four, half), LANES), i16)
 
     solved_shape, p_shape = ((traits, typed), f32), ((typed, half), f32)
@@ -478,8 +486,8 @@
             pltpu.SemaphoreType.DMA((untyped // 128 + 1,)),
         ],
     )
-    x4, gg_own, gp_own = call(
-        pair_backward, [mixed, sq, h4], x1, got1, s_own, x3, got3, g_own, after=(x2,)
+    x4, x4_low, gg_own, gp_own = call(
+        pair_backward, [coded_half, two_coded, sq, h4], x1, got1, s_own, x3, got3, g_own, after=(x2,)
     )
     got2_core = swap(call(relay, coded_half, got2, after=(x4, masked)), 1)
     out = call(group_forward, coded, n_own, got2, got2_core, sp_own)
@@ -487,22 +495,19 @@
     s_group, up, down, n_first, n_second = call(
         group_map, [h4, parts3, parts3, sq, sq], n_own, got2, got2_core, sp_own, after=(out,)
     )
-    k = call(block_map, ((half, typed), f32), n_second, x1, got1, d)
     t_in = jnp.zeros((four, half), f32)
-    got4 = swap(x4, 3)
+    got4, got4_low = swap(x4, 3), swap(x4_low, 3)
     for step in range(groups - 2):
         got = hop(out, step)
         t_in, out = call(
             functools.partial(forward_hop, step), [h4, coded], got, t_in, up, s_group,
-            after=(k,) if step == 0 else (),
+            after=(k,) if step == 1 else (),
         )
         if step == 0:
-            pieces = [((half // 2 + SCALES, LANES), i16)] * 2
-            low, high = call(relay_halves, pieces, got4, after=(out,))
-            got4_low, got4_high = swap(low, 1), swap(high, 1)
+            k = call(block_map, ((half, typed), f32), n_second, x1, got1, d, after=(out,))
     gg_group, g_group, gg_second, g_second = call(
         group_backward, [sq, h4, sq, h4],
-        n_first, got2, sp_own, gg_own, got4, got4_low, got4_high, gp_own, after=(out,),
+        n_first, got2, sp_own, gg_own, got4, got4_low, gp_own, after=(out,),
     )
     last = groups - 2
     got = hop(out, last)

time: 44 us -> 44.3 us (level)
  waiting for transfers between devices: 9.38 us -> 10.7 us
  starting transfers between devices: 19 us -> 17.8 us
    ppermute x14 -> x13, waiting for transfers between devices: 4.67 us -> 7.42 us  [swap(): return lax.ppermute(block, AXIS, [(i, i ^ distance) for i in range(n)])]
    ppermute x6, starting transfers between devices: 7.33 us -> 5.7 us  [hop(): return lax.ppermute(block, AXIS, pairs)]
    ppermute x6, waiting for transfers between devices: 2.02 us -> 0.6 us  [hop(): return lax.ppermute(block, AXIS, pairs)]
    ppermute x14 -> x13, starting transfers between devices: 10.3 us -> 10.6 us  [swap(): return lax.ppermute(block, AXIS, [(i, i ^ distance) for i in range(n)])]
    pallas_call x24 -> x23, Pallas kernels: 14.7 us -> 14.8 us  [call(): pl.pallas_call(body, out_shape=[jax.ShapeDtypeStruct(s, t) if last else p...]
  transfers between devices with their start and end apart: 21 -> 20, of which waited for: 9 -> 9; matrix products, arithmetic and copies ran while one was open for 0% -> 0% of each run, Pallas kernels for 26% -> 25%
where the time goes in v1:
time: 44.3 us; the launch traced here: 43.5 us
  starting transfers between devices  17.8 us (40%)
  Pallas kernels  14.8 us (33%)
  waiting for transfers between devices  10.7 us (24%)
    pallas_call x23, Pallas kernels, call(): pl.pallas_call(body, out_shape=[jax.ShapeDtypeStruct(s, t) if last else p...  14.8 us
    ppermute x13, starting transfers between devices, swap(): return lax.ppermute(block, AXIS, [(i, i ^ distance) for i in range(n)])  10.6 us
    ppermute x13, waiting for transfers between devices, swap(): return lax.ppermute(block, AXIS, [(i, i ^ distance) for i in range(n)])  7.42 us
    ppermute x6, starting transfers between devices, hop(): return lax.ppermute(block, AXIS, pairs)  5.7 us
    ppermute x1, waiting for transfers between devices, swap_chips(): return lax.ppermute(block, (SEGMENTS, AXIS), pairs)  2.71 us
    ppermute x1, starting transfers between devices, swap_chips(): return lax.ppermute(block, (SEGMENTS, AXIS), pairs)  1.46 us
  transfers between devices with their start and end apart: 20, of which 9 were waited for; matrix products, arithmetic and copies ran while one was open for 0% of the time, Pallas kernels for 25%

profile of v1, /device:TPU:1, one launch (start us, length us, event | category | flops | bytes accessed | tf_op | source)
XLA Modules:
  0.0 43.5 jit_solution(6865780941150854426)
XLA Ops:
  0.0 2.1 %tail_part.1 = (f32[384,256]{1,0:T(8,128)S(1)}, f32[128,256]{1,0:T(8,128)S(1)}, f32[256,512]{1,0:T(8,128)S(1)}, f32[512,512]{1,0:T(8,128)S(1)}, f32[512,256]{1,0:T(8,128)S(1)}) custom-call(f32[256,512]{1,0:T(8,128)} %refs_0_.2, f32[512,512]{1,0:T(8,128)} %bitcast.3, f32[512,256]{1,0:T(8,128)} %bitcast.4), custom_call_target="tpu_custom_call" | custom-call | tf_op jit(solution)/shard_map/tail_part/pallas_call | solution.py:100
  2.1 0.1 collective-permute-start
  2.2 1.2 %head_part.1 = (f32[384,256]{1,0:T(8,128)S(1)}, f32[128,256]{1,0:T(8,128)S(1)}, f32[256,512]{1,0:T(8,128)S(1)}, f32[512,256]{1,0:T(8,128)S(1)}) custom-call(f32[256,512]{1,0:T(8,128)S(1)} %get-tuple-element.53.refs_0_, f32[512,512]{1,0:T(8,128)S(1)} %get-tuple-element.54.refs_1_.refs_3_.refs_2_, f32[512,256]{1,0:T(8,128)S(1)} %get-tuple-element.55.refs_2_, ...), custom_call_target="tpu_custom_call" | custom-call | tf_op jit(solution)/shard_map/head_part/pallas_call | solution.py:100
  3.4 0.5 %collective-permute-start.2 = (f32[384,256]{1,0:T(8,128)S(1)}, f32[384,256]{1,0:T(8,128)S(1)}, u32[]{:S(2)}, u32[]{:S(2)}) collective-permute-start(f32[384,256]{1,0:T(8,128)S(1)} %get-tuple-element.59.refs_3_.refs_7_), channel_id=1, source_target_pairs={{0,1},{1,0},{2,3},{3,2},{4,5},{5,4},{6,7},{7,6},{8,9},{9,8},{10,11... | collective-permute-start | bytes 1179656 | tf_op jit(solution)/shard_map/ppermute | solution.py:425
  3.9 0.5 %pair_forward.1 = (s16[416,128]{1,0:T(8,128)(2,1)S(1)}, f32[256,256]{1,0:T(8,128)S(1)}, f32[64,256]{1,0:T(8,128)S(1)}) custom-call(f32[384,256]{1,0:T(8,128)S(1)} %get-tuple-element.51.refs_3_.refs_0_.refs_1_.refs_4_, f32[384,256]{1,0:T(8,128)S(1)} %collective-permute-done.refs_1_.refs_2_.refs_5_, f32[128,256]{1,0:T(8,128)S(1)} %get-tuple-element.52.refs_4_.refs_2_.refs_6_, ...), custom_call_target="tpu_custom_call" | custom-call | tf_op jit(solution)/shard_map/pair_forward/pallas_call | solution.py:100
  4.4 2.7 %collective-permute-start.1 = (s16[416,128]{1,0:T(8,128)(2,1)S(1)}, s16[416,128]{1,0:T(8,128)(2,1)S(1)}, u32[]{:S(2)}, u32[]{:S(2)}) collective-permute-start(s16[416,128]{1,0:T(8,128)(2,1)S(1)} %get-tuple-element.58.refs_6_.refs_2_), channel_id=1, source_target_pairs={{0,3},{1,2},{2,1},{3,0},{4,7},{5,6},{6,5},{7,4},{8,11},{9,10},{10,... | collective-permute-start | bytes 319496 | tf_op jit(solution)/shard_map/ppermute | solution.py:425
  7.1 1.7 %mask_coefs.1.refs_2_.refs_3_ = bf16[512,1024]{1,0:T(8,128)(2,1)S(1)} custom-call(bf16[512,1024]{1,0:T(8,128)(2,1)} %refs_0_.3, s32[1,512]{1,0:T(1,128)} %bitcast.5, s16[416,128]{1,0:T(8,128)(2,1)S(1)} %get-tuple-element.58.refs_6_.refs_2_), custom_call_target="tpu_custom_call" | custom-call | tf_op jit(solution)/shard_map/mask_coefs/pallas_call | solution.py:100
  8.8 1.0 %pair_backward.1 = (s16[272,128]{1,0:T(8,128)(2,1)S(1)}, s16[288,128]{1,0:T(8,128)(2,1)S(1)}, f32[256,256]{1,0:T(8,128)S(1)}, f32[64,256]{1,0:T(8,128)S(1)}) custom-call(f32[384,256]{1,0:T(8,128)S(1)} %get-tuple-element.51.refs_3_.refs_0_.refs_1_.refs_4_, f32[384,256]{1,0:T(8,128)S(1)} %collective-permute-done.refs_1_.refs_2_.refs_5_, ...), custom_call_target="tpu_custom_call" | custom-call | tf_op jit(solution)/shard_map/pair_backward/pallas_call | solution.py:100
  9.9 0.1 collective-permute-done.1.refs_0_.refs_1_.refs_2_
  10.0 0.3 collective-permute-start.3
  10.3 1.0 %collective-permute-done.3.refs_2_ = s16[272,128]{1,0:T(8,128)(2,1)S(1)} collective-permute-done((s16[272,128]{1,0:T(8,128)(2,1)S(1)}, s16[272,128]{1,0:T(8,128)(2,1)S(1)}, u32[]{:S(2)}, u32[]{:S(2)}) %collective-permute-start.3) | collective-permute-done | bytes 69664 | tf_op jit(solution)/shard_map/ppermute | solution.py:425
  11.3 0.3 group_forward.1.refs_4_
  11.6 1.8 %collective-permute-start.4 = (s16[144,128]{1,0:T(8,128)(2,1)S(1)}, s16[144,128]{1,0:T(8,128)(2,1)S(1)}, u32[]{:S(2)}, u32[]{:S(2)}) collective-permute-start(s16[144,128]{1,0:T(8,128)(2,1)S(1)} %group_forward.1.refs_4_), channel_id=1, source_target_pairs={{0,5},{1,4},{2,7},{3,6},{4,1},{5,0},{6,3},{7,2},{8,9},{9,8},{10,11... | collective-permute-start | bytes 110600 | tf_op jit(solution)/shard_map/ppermute | solution.py:434
  13.5 1.3 %collective-permute-start.8 = (s16[288,128]{1,0:T(8,128)(2,1)S(1)}, s16[288,128]{1,0:T(8,128)(2,1)S(1)}, u32[]{:S(2)}, u32[]{:S(2)}) collective-permute-start(s16[288,128]{1,0:T(8,128)(2,1)S(1)} %get-tuple-element.72), channel_id=1, source_target_pairs={{0,3},{1,2},{2,1},{3,0},{4,7},{5,6},{6,5},{7,4},{8,11},{9,10},{10,... | collective-permute-start | bytes 221192 | tf_op jit(solution)/shard_map/ppermute | solution.py:425
  14.7 0.5 %group_map.1 = (f32[64,256]{1,0:T(8,128)S(1)}, bf16[768,256]{1,0:T(8,128)(2,1)S(1)}, bf16[768,256]{1,0:T(8,128)(2,1)S(1)}, f32[256,256]{1,0:T(8,128)S(1)}, f32[256,256]{1,0:T(8,128)S(1)}) custom-call(f32[256,256]{1,0:T(8,128)S(1)} %get-tuple-element.57.refs_0_, s16[416,128]{1,0:T(8,128)(2,1)S(1)} %collective-permute-done.1.refs_0_.refs_1_.refs_2_, ...), custom_call_target="tpu_custom_call" | custom-call | tf_op jit(solution)/shard_map/group_map/pallas_call | solution.py:100
  15.3 0.2 forward_hop.2
  15.5 0.4 collective-permute-start.5
  15.9 1.8 %collective-permute-start.7 = (s16[272,128]{1,0:T(8,128)(2,1)S(1)}, s16[272,128]{1,0:T(8,128)(2,1)S(1)}, u32[]{:S(2)}, u32[]{:S(2)}) collective-permute-start(s16[272,128]{1,0:T(8,128)(2,1)S(1)} %get-tuple-element.61.refs_1_), channel_id=1, source_target_pairs={{0,3},{1,2},{2,1},{3,0},{4,7},{5,6},{6,5},{7,4},{8,11},{9,10},{10,... | collective-permute-start | bytes 208904 | tf_op jit(solution)/shard_map/ppermute | solution.py:425
  17.7 0.6 %block_map.1.refs_4_.refs_5_ = f32[256,512]{1,0:T(8,128)S(1)} custom-call(f32[256,256]{1,0:T(8,128)S(1)} %get-tuple-element.67.refs_0_, f32[384,256]{1,0:T(8,128)S(1)} %get-tuple-element.51.refs_3_.refs_0_.refs_1_.refs_4_, f32[384,256]{1,0:T(8,128)S(1)} %collective-permute-done.refs_1_.refs_2_.refs_5_, ...), custom_call_target="tpu_custom_call" | custom-call | tf_op jit(solution)/shard_map/block_map/pallas_call | solution.py:100
  18.3 0.2 forward_hop.3
  18.6 0.4 collective-permute-start.6
  19.0 1.1 %collective-permute-done.7.refs_4_ = s16[272,128]{1,0:T(8,128)(2,1)S(1)} collective-permute-done((s16[272,128]{1,0:T(8,128)(2,1)S(1)}, s16[272,128]{1,0:T(8,128)(2,1)S(1)}, u32[]{:S(2)}, u32[]{:S(2)}) %collective-permute-start.7) | collective-permute-done | bytes 69664 | tf_op jit(solution)/shard_map/ppermute | solution.py:425
  20.1 0.9 %group_backward.1 = (f32[256,256]{1,0:T(8,128)S(1)}, f32[64,256]{1,0:T(8,128)S(1)}, f32[256,256]{1,0:T(8,128)S(1)}, f32[64,256]{1,0:T(8,128)S(1)}) custom-call(f32[256,256]{1,0:T(8,128)S(1)} %get-tuple-element.70.refs_0_.refs_1_, s16[416,128]{1,0:T(8,128)(2,1)S(1)} %collective-permute-done.1.refs_0_.refs_1_.refs_2_, ...), custom_call_target="tpu_custom_call" | custom-call | tf_op jit(solution)/shard_map/group_backward/pallas_call | solution.py:100
  21.1 0.4 collective-permute-start.9
  21.5 0.6 %spread_forward.1 = (s16[144,128]{1,0:T(8,128)(2,1)S(1)}, s16[144,128]{1,0:T(8,128)(2,1)S(1)}, f32[64,256]{1,0:T(8,128)S(1)}, f32[64,256]{1,0:T(8,128)S(1)}, f32[64,256]{1,0:T(8,128)S(1)}) custom-call(f32[64,256]{1,0:T(8,128)S(1)} %get-tuple-element.78.refs_0_, f32[256,256]{1,0:T(8,128)S(1)} %get-tuple-element.70.refs_0_.refs_1_, ...), custom_call_target="tpu_custom_call" | custom-call | tf_op jit(solution)/shard_map/spread_forward/pallas_call | solution.py:100
  22.2 1.6 %collective-permute-start.15 = (s16[144,128]{1,0:T(8,128)(2,1)S(1)}, s16[144,128]{1,0:T(8,128)(2,1)S(1)}, u32[]{:S(2)}, u32[]{:S(2)}) collective-permute-start(s16[144,128]{1,0:T(8,128)(2,1)S(1)} %get-tuple-element.90), channel_id=1, source_target_pairs={{0,3},{1,2},{2,1},{3,0},{4,7},{5,6},{6,5},{7,4},{8,11},{9,10},{10,... | collective-permute-start | bytes 110600 | tf_op jit(solution)/shard_map/ppermute | solution.py:425
  23.8 0.2 collective-permute-start.16
  24.0 0.2 backward_hop.2
  24.2 0.2 collective-permute-start.10
  24.5 1.2 %collective-permute-done.15.refs_2_ = s16[144,128]{1,0:T(8,128)(2,1)S(1)} collective-permute-done((s16[144,128]{1,0:T(8,128)(2,1)S(1)}, s16[144,128]{1,0:T(8,128)(2,1)S(1)}, u32[]{:S(2)}, u32[]{:S(2)}) %collective-permute-start.15) | collective-permute-done | bytes 36896 | tf_op jit(solution)/shard_map/ppermute | solution.py:425
  25.6 1.6 %collective-permute-done.16.refs_3_ = s16[144,128]{1,0:T(8,128)(2,1)S(1)} collective-permute-done((s16[144,128]{1,0:T(8,128)(2,1)S(1)}, s16[144,128]{1,0:T(8,128)(2,1)S(1)}, u32[]{:S(2)}, u32[]{:S(2)}) %collective-permute-start.16) | collective-permute-done | bytes 36896 | tf_op jit(solution)/shard_map/ppermute | solution.py:425
  27.2 0.7 %pair_states.1 = (s16[544,128]{1,0:T(8,128)(2,1)S(1)}, f32[256,256]{1,0:T(8,128)S(1)}) custom-call(f32[64,256]{1,0:T(8,128)S(1)} %get-tuple-element.88.refs_0_, f32[64,256]{1,0:T(8,128)S(1)} %get-tuple-element.89.refs_1_, s16[144,128]{1,0:T(8,128)(2,1)S(1)} %collective-permute-done.15.refs_2_, s16[144,128]{1,0:T(8,128)(2,1)S(1)} %collective-permute-done.16.refs_3_, ...), custom_call_target="tpu_custom_call" | custom-call | tf_op jit(solution)/shard_map/pair_states/pallas_call | solution.py:100
  27.8 0.3 collective-permute-start.17
  28.1 0.2 backward_hop.3
  28.4 2.4 %collective-permute-start.11 = (s16[144,128]{1,0:T(8,128)(2,1)S(1)}, s16[144,128]{1,0:T(8,128)(2,1)S(1)}, u32[]{:S(2)}, u32[]{:S(2)}) collective-permute-start(s16[144,128]{1,0:T(8,128)(2,1)S(1)} %get-tuple-element.84.refs_3_), channel_id=1, source_target_pairs={{0,5},{1,4},{2,7},{3,6},{4,1},{5,0},{6,3},{7,2},{8,9},{9,8},{10,11... | collective-permute-start | bytes 110600 | tf_op jit(solution)/shard_map/ppermute | solution.py:434
  30.8 1.1 %block_parts.1 = (f32[256,512]{1,0:T(8,128)S(1)}, f32[512,512]{1,0:T(8,128)S(1)}) custom-call(f32[256,512]{1,0:T(8,128)S(1)} %get-tuple-element.86.refs_0_, f32[512,256]{1,0:T(8,128)S(1)} %get-tuple-element.56.refs_3_.refs_1_, f32[512,512]{1,0:T(8,128)S(1)} %get-tuple-element.54.refs_1_.refs_3_.refs_2_, s16[144,128]{1,0:T(8,128)(2,1)S(1)} %get-tuple-element.84.refs_3_), custom_call_target="tpu_custom_call" | custom-call | tf_op jit(solution)/shard_map/block_parts/pallas_call | solution.py:100
  31.8 0.6 %collective-permute-done.11.refs_0_ = s16[144,128]{1,0:T(8,128)(2,1)S(1)} collective-permute-done((s16[144,128]{1,0:T(8,128)(2,1)S(1)}, s16[144,128]{1,0:T(8,128)(2,1)S(1)}, u32[]{:S(2)}, u32[]{:S(2)}) %collective-permute-start.11) | collective-permute-done | bytes 36896 | tf_op jit(solution)/shard_map/ppermute | solution.py:434
  32.5 1.4 %collective-permute-start.12 = (s16[144,128]{1,0:T(8,128)(2,1)S(1)}, s16[144,128]{1,0:T(8,128)(2,1)S(1)}, u32[]{:S(2)}, u32[]{:S(2)}) collective-permute-start(s16[144,128]{1,0:T(8,128)(2,1)S(1)} %arrive.1.refs_0_), channel_id=1, source_target_pairs={{0,3},{1,2},{2,1},{3,0},{4,7},{5,6},{6,5},{7,4},{8,11},{9,10},{10,... | collective-permute-start | bytes 110600 | tf_op jit(solution)/shard_map/ppermute | solution.py:425
  33.9 0.1 collective-permute-start.13
  34.0 2.0 %collective-permute-done.12.refs_1_ = s16[144,128]{1,0:T(8,128)(2,1)S(1)} collective-permute-done((s16[144,128]{1,0:T(8,128)(2,1)S(1)}, s16[144,128]{1,0:T(8,128)(2,1)S(1)}, u32[]{:S(2)}, u32[]{:S(2)}) %collective-permute-start.12) | collective-permute-done | bytes 36896 | tf_op jit(solution)/shard_map/ppermute | solution.py:425
  36.1 0.7 %block_fixed.1.refs_4_ = f32[256,512]{1,0:T(8,128)S(1)} custom-call(f32[256,256]{1,0:T(8,128)S(1)} %get-tuple-element.92.refs_0_, s16[544,128]{1,0:T(8,128)(2,1)S(1)} %collective-permute-done.17.refs_1_, f32[256,512]{1,0:T(8,128)S(1)} %get-tuple-element.94.refs_2_, f32[512,512]{1,0:T(8,128)S(1)} %get-tuple-element.87.refs_2_.refs_3_), custom_call_target="tpu_custom_call" | custom-call | tf_op jit(solution)/shard_map/block_fixed/pallas_call | solution.py:100
  36.7 0.5 %collective-permute-done.14.refs_3_ = s16[144,128]{1,0:T(8,128)(2,1)S(1)} collective-permute-done((s16[144,128]{1,0:T(8,128)(2,1)S(1)}, s16[144,128]{1,0:T(8,128)(2,1)S(1)}, u32[]{:S(2)}, u32[]{:S(2)}) %collective-permute-start.14) | collective-permute-done | bytes 36896 | tf_op jit(solution)/shard_map/ppermute | solution.py:425
  37.2 0.4 block_weights.1
  37.6 1.5 %collective-permute-start.18 = (bf16[256,256]{1,0:T(8,128)(2,1)S(1)}, bf16[256,256]{1,0:T(8,128)(2,1)S(1)}, u32[]{:S(2)}, u32[]{:S(2)}) collective-permute-start(bf16[256,256]{1,0:T(8,128)(2,1)S(1)} %get-tuple-element.95.refs_0_), channel_id=1, source_target_pairs={{0,16},{1,2},{2,1},{3,4},{4,3},{5,6},{6,5},{7,8},{8,7},{9,10},{10,... | collective-permute-start | bytes 393224 | tf_op jit(solution)/shard_map/ppermute | solution.py:446
  39.1 0.2 collective-permute-start.19
  39.3 0.3 impute_own.1.refs_0_
  39.7 2.7 %collective-permute-done.18.refs_1_ = bf16[256,256]{1,0:T(8,128)(2,1)S(1)} collective-permute-done((bf16[256,256]{1,0:T(8,128)(2,1)S(1)}, bf16[256,256]{1,0:T(8,128)(2,1)S(1)}, u32[]{:S(2)}, u32[]{:S(2)}) %collective-permute-start.18) | collective-permute-done | bytes 131104 | tf_op jit(solution)/shard_map/ppermute | solution.py:446
  42.4 1.1 %impute_edges.1 = f32[256,512]{1,0:T(8,128)} custom-call(f32[256,512]{1,0:T(8,128)S(1)} %impute_own.1.refs_0_, bf16[256,256]{1,0:T(8,128)(2,1)S(1)} %collective-permute-done.18.refs_1_, bf16[256,256]{1,0:T(8,128)(2,1)S(1)} %collective-permute-done.19.refs_2_, bf16[512,1024]{1,0:T(8,128)(2,1)S(1)} %mask_coefs.1.refs_2_.refs_3_), custom_call_target="tpu_custom_call" | custom-call | tf_op jit(solution)/shard_map/impute_edges/pallas_call | solution.py:100
  (16 shorter events, 0.2 us)
Async XLA Ops:
  2.1 1.9 %collective-permute-start = (f32[384,256]{1,0:T(8,128)S(1)}, f32[384,256]{1,0:T(8,128)S(1)}, u32[]{:S(2)}, u32[]{:S(2)}) collective-permute-start(f32[384,256]{1,0:T(8,128)S(1)} %get-tuple-element.51.refs_3_.refs_0_.refs_1_.refs_4_), channel_id=1, source_target_pairs={{0,1},{1,0},{2,3},{3,2},{4,5},{5,4},{6,7},{7,6},{8,9},{9,8},{10,11... | collective-permute-start | bytes 1179656 | tf_op jit(solution)/shard_map/ppermute | solution.py:425
  3.4 5.4 %collective-permute-start.2 = (f32[384,256]{1,0:T(8,128)S(1)}, f32[384,256]{1,0:T(8,128)S(1)}, u32[]{:S(2)}, u32[]{:S(2)}) collective-permute-start(f32[384,256]{1,0:T(8,128)S(1)} %get-tuple-element.59.refs_3_.refs_7_), channel_id=1, source_target_pairs={{0,1},{1,0},{2,3},{3,2},{4,5},{5,4},{6,7},{7,6},{8,9},{9,8},{10,11... | collective-permute-start | bytes 1179656 | tf_op jit(solution)/shard_map/ppermute | solution.py:425
  4.4 5.6 %collective-permute-start.1 = (s16[416,128]{1,0:T(8,128)(2,1)S(1)}, s16[416,128]{1,0:T(8,128)(2,1)S(1)}, u32[]{:S(2)}, u32[]{:S(2)}) collective-permute-start(s16[416,128]{1,0:T(8,128)(2,1)S(1)} %get-tuple-element.58.refs_6_.refs_2_), channel_id=1, source_target_pairs={{0,3},{1,2},{2,1},{3,0},{4,7},{5,6},{6,5},{7,4},{8,11},{9,10},{10,... | collective-permute-start | bytes 319496 | tf_op jit(solution)/shard_map/ppermute | solution.py:425
  10.0 1.3 %collective-permute-start.3 = (s16[272,128]{1,0:T(8,128)(2,1)S(1)}, s16[272,128]{1,0:T(8,128)(2,1)S(1)}, u32[]{:S(2)}, u32[]{:S(2)}) collective-permute-start(s16[272,128]{1,0:T(8,128)(2,1)S(1)} %relay.1), channel_id=1, source_target_pairs={{0,1},{1,0},{2,3},{3,2},{4,5},{5,4},{6,7},{7,6},{8,9},{9,8},{10,11... | collective-permute-start | bytes 208904 | tf_op jit(solution)/shard_map/ppermute | solution.py:425
  11.6 3.6 %collective-permute-start.4 = (s16[144,128]{1,0:T(8,128)(2,1)S(1)}, s16[144,128]{1,0:T(8,128)(2,1)S(1)}, u32[]{:S(2)}, u32[]{:S(2)}) collective-permute-start(s16[144,128]{1,0:T(8,128)(2,1)S(1)} %group_forward.1.refs_4_), channel_id=1, source_target_pairs={{0,5},{1,4},{2,7},{3,6},{4,1},{5,0},{6,3},{7,2},{8,9},{9,8},{10,11... | collective-permute-start | bytes 110600 | tf_op jit(solution)/shard_map/ppermute | solution.py:434
  13.5 6.7 %collective-permute-start.8 = (s16[288,128]{1,0:T(8,128)(2,1)S(1)}, s16[288,128]{1,0:T(8,128)(2,1)S(1)}, u32[]{:S(2)}, u32[]{:S(2)}) collective-permute-start(s16[288,128]{1,0:T(8,128)(2,1)S(1)} %get-tuple-element.72), channel_id=1, source_target_pairs={{0,3},{1,2},{2,1},{3,0},{4,7},{5,6},{6,5},{7,4},{8,11},{9,10},{10,... | collective-permute-start | bytes 221192 | tf_op jit(solution)/shard_map/ppermute | solution.py:425
  15.5 2.8 %collective-permute-start.5 = (s16[144,128]{1,0:T(8,128)(2,1)S(1)}, s16[144,128]{1,0:T(8,128)(2,1)S(1)}, u32[]{:S(2)}, u32[]{:S(2)}) collective-permute-start(s16[144,128]{1,0:T(8,128)(2,1)S(1)} %get-tuple-element.65.refs_4_), channel_id=1, source_target_pairs={{0,1},{1,0},{2,3},{3,2},{4,9},{5,8},{6,11},{7,10},{8,5},{9,4},{10,... | collective-permute-start | bytes 110600 | tf_op jit(solution)/shard_map/ppermute | solution.py:434
  15.9 4.2 %collective-permute-start.7 = (s16[272,128]{1,0:T(8,128)(2,1)S(1)}, s16[272,128]{1,0:T(8,128)(2,1)S(1)}, u32[]{:S(2)}, u32[]{:S(2)}) collective-permute-start(s16[272,128]{1,0:T(8,128)(2,1)S(1)} %get-tuple-element.61.refs_1_), channel_id=1, source_target_pairs={{0,3},{1,2},{2,1},{3,0},{4,7},{5,6},{6,5},{7,4},{8,11},{9,10},{10,... | collective-permute-start | bytes 208904 | tf_op jit(solution)/shard_map/ppermute | solution.py:425
  18.6 2.5 %collective-permute-start.6 = (s16[144,128]{1,0:T(8,128)(2,1)S(1)}, s16[144,128]{1,0:T(8,128)(2,1)S(1)}, u32[]{:S(2)}, u32[]{:S(2)}) collective-permute-start(s16[144,128]{1,0:T(8,128)(2,1)S(1)} %get-tuple-element.68.refs_7_), channel_id=1, source_target_pairs={{0,1},{1,0},{2,3},{3,2},{4,5},{5,4},{6,7},{7,6},{8,13},{9,12},{10,... | collective-permute-start | bytes 110600 | tf_op jit(solution)/shard_map/ppermute | solution.py:434
  21.1 2.9 %collective-permute-start.9 = (s16[144,128]{1,0:T(8,128)(2,1)S(1)}, s16[144,128]{1,0:T(8,128)(2,1)S(1)}, u32[]{:S(2)}, u32[]{:S(2)}) collective-permute-start(s16[144,128]{1,0:T(8,128)(2,1)S(1)} %get-tuple-element.76.refs_8_), channel_id=1, source_target_pairs={{0,1},{1,0},{2,3},{3,2},{4,5},{5,4},{6,7},{7,6},{8,13},{9,12},{10,... | collective-permute-start | bytes 110600 | tf_op jit(solution)/shard_map/ppermute | solution.py:434
  22.2 3.4 %collective-permute-start.15 = (s16[144,128]{1,0:T(8,128)(2,1)S(1)}, s16[144,128]{1,0:T(8,128)(2,1)S(1)}, u32[]{:S(2)}, u32[]{:S(2)}) collective-permute-start(s16[144,128]{1,0:T(8,128)(2,1)S(1)} %get-tuple-element.90), channel_id=1, source_target_pairs={{0,3},{1,2},{2,1},{3,0},{4,7},{5,6},{6,5},{7,4},{8,11},{9,10},{10,... | collective-permute-start | bytes 110600 | tf_op jit(solution)/shard_map/ppermute | solution.py:425
  23.8 3.4 %collective-permute-start.16 = (s16[144,128]{1,0:T(8,128)(2,1)S(1)}, s16[144,128]{1,0:T(8,128)(2,1)S(1)}, u32[]{:S(2)}, u32[]{:S(2)}) collective-permute-start(s16[144,128]{1,0:T(8,128)(2,1)S(1)} %get-tuple-element.91), channel_id=1, source_target_pairs={{0,3},{1,2},{2,1},{3,0},{4,7},{5,6},{6,5},{7,4},{8,11},{9,10},{10,... | collective-permute-start | bytes 110600 | tf_op jit(solution)/shard_map/ppermute | solution.py:425
  24.2 3.9 %collective-permute-start.10 = (s16[144,128]{1,0:T(8,128)(2,1)S(1)}, s16[144,128]{1,0:T(8,128)(2,1)S(1)}, u32[]{:S(2)}, u32[]{:S(2)}) collective-permute-start(s16[144,128]{1,0:T(8,128)(2,1)S(1)} %get-tuple-element.82), channel_id=1, source_target_pairs={{0,1},{1,0},{2,3},{3,2},{4,9},{5,8},{6,11},{7,10},{8,5},{9,4},{10,... | collective-permute-start | bytes 110600 | tf_op jit(solution)/shard_map/ppermute | solution.py:434
  27.8 8.2 %collective-permute-start.17 = (s16[544,128]{1,0:T(8,128)(2,1)S(1)}, s16[544,128]{1,0:T(8,128)(2,1)S(1)}, u32[]{:S(2)}, u32[]{:S(2)}) collective-permute-start(s16[544,128]{1,0:T(8,128)(2,1)S(1)} %get-tuple-element.93), channel_id=1, source_target_pairs={{0,1},{1,0},{2,3},{3,2},{4,5},{5,4},{6,7},{7,6},{8,9},{9,8},{10,11... | collective-permute-start | bytes 417800 | tf_op jit(solution)/shard_map/ppermute | solution.py:425
  28.4 4.0 %collective-permute-start.11 = (s16[144,128]{1,0:T(8,128)(2,1)S(1)}, s16[144,128]{1,0:T(8,128)(2,1)S(1)}, u32[]{:S(2)}, u32[]{:S(2)}) collective-permute-start(s16[144,128]{1,0:T(8,128)(2,1)S(1)} %get-tuple-element.84.refs_3_), channel_id=1, source_target_pairs={{0,5},{1,4},{2,7},{3,6},{4,1},{5,0},{6,3},{7,2},{8,9},{9,8},{10,11... | collective-permute-start | bytes 110600 | tf_op jit(solution)/shard_map/ppermute | solution.py:434
  32.5 3.5 %collective-permute-start.12 = (s16[144,128]{1,0:T(8,128)(2,1)S(1)}, s16[144,128]{1,0:T(8,128)(2,1)S(1)}, u32[]{:S(2)}, u32[]{:S(2)}) collective-permute-start(s16[144,128]{1,0:T(8,128)(2,1)S(1)} %arrive.1.refs_0_), channel_id=1, source_target_pairs={{0,3},{1,2},{2,1},{3,0},{4,7},{5,6},{6,5},{7,4},{8,11},{9,10},{10,... | collective-permute-start | bytes 110600 | tf_op jit(solution)/shard_map/ppermute | solution.py:425
  33.9 2.8 %collective-permute-start.13 = (s16[144,128]{1,0:T(8,128)(2,1)S(1)}, s16[144,128]{1,0:T(8,128)(2,1)S(1)}, u32[]{:S(2)}, u32[]{:S(2)}) collective-permute-start(s16[144,128]{1,0:T(8,128)(2,1)S(1)} %arrive.1.refs_0_), channel_id=1, source_target_pairs={{0,1},{1,0},{2,3},{3,2},{4,5},{5,4},{6,7},{7,6},{8,9},{9,8},{10,11... | collective-permute-start | bytes 110600 | tf_op jit(solution)/shard_map/ppermute | solution.py:425
  36.0 1.2 %collective-permute-start.14 = (s16[144,128]{1,0:T(8,128)(2,1)S(1)}, s16[144,128]{1,0:T(8,128)(2,1)S(1)}, u32[]{:S(2)}, u32[]{:S(2)}) collective-permute-start(s16[144,128]{1,0:T(8,128)(2,1)S(1)} %collective-permute-done.12.refs_1_), channel_id=1, source_target_pairs={{0,1},{1,0},{2,3},{3,2},{4,5},{5,4},{6,7},{7,6},{8,9},{9,8},{10,11... | collective-permute-start | bytes 110600 | tf_op jit(solution)/shard_map/ppermute | solution.py:425
  37.6 4.8 %collective-permute-start.18 = (bf16[256,256]{1,0:T(8,128)(2,1)S(1)}, bf16[256,256]{1,0:T(8,128)(2,1)S(1)}, u32[]{:S(2)}, u32[]{:S(2)}) collective-permute-start(bf16[256,256]{1,0:T(8,128)(2,1)S(1)} %get-tuple-element.95.refs_0_), channel_id=1, source_target_pairs={{0,16},{1,2},{2,1},{3,4},{4,3},{5,6},{6,5},{7,8},{8,7},{9,10},{10,... | collective-permute-start | bytes 393224 | tf_op jit(solution)/shard_map/ppermute | solution.py:446
  39.1 3.3 %collective-permute-start.19 = (bf16[256,256]{1,0:T(8,128)(2,1)S(1)}, bf16[256,256]{1,0:T(8,128)(2,1)S(1)}, u32[]{:S(2)}, u32[]{:S(2)}) collective-permute-start(bf16[256,256]{1,0:T(8,128)(2,1)S(1)} %get-tuple-element.96.refs_1_), channel_id=1, source_target_pairs={{0,1},{1,0},{2,3},{3,2},{4,5},{5,4},{6,7},{7,6},{8,9},{9,8},{10,11... | collective-permute-start | bytes 393224 | tf_op jit(solution)/shard_map/ppermute | solution.py:425
